TPU v7x, 32 devices: a whole 2x2x4 slice. The times are simulated.
32 devices in a mesh: tp: 4 (over y, x), lat: 8 (over z, core).
Axes of the slice: x: 2, y: 2, z: 4, core: 2. Of those that a mesh axis runs over, the one named last changes fastest.
Arguments:
- attn_out: bfloat16 [512, 2048], P('lat', 'tp'), may hold values from -6 to 6
- w_out: bfloat16 [2048, 8192], P('tp'), may hold values from -0.125 to 0.125
- resid_in: bfloat16 [512, 8192], P(('lat', 'tp')), may hold values from -6 to 6
- positions: int32 [64], replicated, may hold values from 0 to 511
- w_enc: bfloat16 [8192, 32768], P(None, ('tp', 'lat')), may hold values from -0.0625 to 0.0625
- b_enc: float32 [32768], P(('tp', 'lat')), may hold values from -3 to 3
- dec_norm: float32 [32768], P(('tp', 'lat')), may hold values from 0.05 to 0.5
- b_dec: float32 [8192], replicated, may hold values from -3 to 3
Outputs:
- stream: bfloat16 [512, 8192], P(('lat', 'tp'))
- codes: bfloat16 [64, 32768], P(None, ('tp', 'lat'))
- recon: bfloat16 [64, 8192], P(('tp', 'lat'))
- error: float32 [64], P(('tp', 'lat'))
All inputs are finite; a program needn't handle non-finite values.
Results may differ from a plain program's by a relative error of at most 0.0059.
Values may be sent and summed in bfloat16 or wider, within the bound.
A program may use at most 128 MiB of HBM per device.

v0:
```python
import jax
import jax.numpy as jnp
from jax import lax
from jax.sharding import PartitionSpec as P


def shards(attn_out, w_out, resid_in, positions, w_enc, b_enc, dec_norm, b_dec):
    n_tp = lax.axis_size("tp")
    n_lat = lax.axis_size("lat")
    own_rows = resid_in.shape[0]
    sel_rows = positions.shape[0]
    share_rows = sel_rows // (n_tp * n_lat)
    block = attn_out
    mixed = lax.psum_scatter(
        jnp.dot(block, w_out, preferred_element_type=jnp.float32),
        "tp",
        scatter_dimension=0,
        tiled=True,
    )
    stream = (resid_in.astype(jnp.float32) + mixed).astype(jnp.bfloat16)
    base = (lax.axis_index("lat") * n_tp + lax.axis_index("tp")) * own_rows
    local_ids = base + lax.iota(jnp.int32, own_rows)
    onehot = (positions[:, None] == local_ids[None, :]).astype(jnp.bfloat16)
    owned = jnp.dot(onehot, stream, preferred_element_type=jnp.float32)
    picked = lax.psum(owned, ("tp", "lat")).astype(jnp.bfloat16)
    centered = (picked.astype(jnp.float32) - b_dec).astype(jnp.bfloat16)
    pre = jnp.dot(centered, w_enc, preferred_element_type=jnp.float32) + b_enc
    codes = (jnp.maximum(pre, 0.0) * dec_norm).astype(jnp.bfloat16)
    block = codes
    partial_tp = lax.psum_scatter(
        lax.dot_general(block, w_enc, (((1,), (1,)), ((), ())), preferred_element_type=jnp.float32),
        "tp",
        scatter_dimension=0,
        tiled=True,
    )
    summed = lax.psum_scatter(partial_tp, "lat", scatter_dimension=0, tiled=True)
    full = summed + b_dec
    first = (lax.axis_index("tp") * n_lat + lax.axis_index("lat")) * share_rows
    mine = lax.dynamic_slice_in_dim(picked, first, share_rows, 0).astype(jnp.float32)
    error = jnp.mean((full - mine) ** 2, axis=1)
    return (stream, codes, full.astype(jnp.bfloat16), error)


def solution(mesh):
    placed = (
        P("lat", "tp"),
        P("tp", None),
        P(("lat", "tp"), None),
        P(),
        P(None, ("tp", "lat")),
        P(("tp", "lat")),
        P(("tp", "lat")),
        P(),
    )
    return jax.shard_map(
        shards,
        mesh=mesh,
        in_specs=placed,
        out_specs=(
            P(("lat", "tp"), None),
            P(None, ("tp", "lat")),
            P(("tp", "lat"), None),
            P(("tp", "lat")),
        ),
        check_vma=False,
    )
```

profile of v0, /device:TPU:0, one launch (start us, length us, event | category | flops | bytes accessed | tf_op | source)
XLA Modules:
  0.0 239.2 jit_solution(1884604794131839034)
XLA Ops:
  7.2 0.0 copy-start
  7.2 0.0 copy-start.3
  7.2 0.0 copy-start.7
  7.2 0.0 copy-start.6
  7.2 0.0 copy-start.5
  7.2 0.0 copy-start.4
  7.2 0.0 reduce-scatter.3.cloned.1.call-start
  7.3 0.7 copy-done
  8.0 6.3 %fusion.9 = f32[64,8192]{1,0:T(8,128)} fusion(bf16[64,512]{1,0:T(8,128)(2,1)S(1)} %copy-done, bf16[512,8192]{1,0:T(8,128)(2,1)} %param.9), kind=kOutput, calls=%fused_computation.16 | convolution fusion | flops 536870912 | bytes 10551296 | tf_op jit(solution)/shard_map/dot_general | solution.py:15
  14.3 0.0 reduce-scatter.3.cloned.1.call-update
  14.3 0.0 reduce-scatter.5.cloned.1.call-start
  14.4 38.0 %reduce-scatter.3.cloned.1.call-done = f32[16,8192]{1,0:T(8,128)} async-done(((f32[64,8192]{1,0:T(8,128)}), f32[16,8192]{1,0:T(8,128)}) %reduce-scatter.3.cloned.1.call-update) | async-done | bytes 524304 | tf_op jit(solution)/shard_map/reduce_scatter | solution.py:14
  52.4 0.0 copy-done.3
  52.4 1.1 add_convert_fusion
  53.5 0.0 copy-done.7
  53.5 0.0 copy-start.1
  53.5 0.5 fusion.5
  54.0 62.2 %all-reduce.5 = bf16[64,8192]{1,0:T(8,128)(2,1)S(1)} all-reduce(f32[64,8192]{1,0:T(8,128)S(1)} %fusion.5), channel_id=1, replica_groups=mesh['tp'=4,'lat'=8] {'tp','lat'}, use_global_device_ids=true, to_apply=%region_1.0 | all-reduce | flops 524288 | bytes 3145728 | tf_op jit(solution)/shard_map/psum | solution.py:25
  116.1 0.0 copy-done.6
  116.1 0.0 copy-done.5
  116.1 0.0 copy-done.4
  116.2 8.8 %fusion.2 = bf16[64,1024]{1,0:T(8,128)(2,1)S(1)} fusion(bf16[8192,1024]{1,0:T(8,128)(2,1)} %param.12, bf16[64,8192]{1,0:T(8,128)(2,1)S(1)} %all-reduce.5, f32[8192]{0:T(1024)S(1)} %copy-done.4, f32[1024]{0:T(1024)S(1)} %copy-done.5, f32[1024]{0:T(1024)S(1)} %copy-done.6), kind=kOutput, calls=%fused_computation.4 | convolution fusion | flops 1075576832 | bytes 17997824 | tf_op jit(solution)/shard_map/dot_general | solution.py:27
  125.0 0.0 copy-done.1
  125.0 0.0 copy-start.2
  125.0 0.0 copy-start.8
  125.0 12.3 %fusion.10 = f32[64,8192]{1,0:T(8,128)} fusion(bf16[64,1024]{1,0:T(8,128)(2,1)S(1)} %fusion.2, bf16[8192,1024]{1,0:T(8,128)(2,1)} %param.12), kind=kOutput, calls=%fused_computation.17 | convolution fusion | flops 1073741824 | bytes 19005440 | tf_op jit(solution)/shard_map/dot_general | solution.py:31
  137.3 0.0 copy-done.2
  137.3 0.0 reduce-scatter.5.cloned.1.call-update
  137.4 0.0 all-reduce.4.cloned.1.call-start
  137.4 34.5 %reduce-scatter.5.cloned.1.call-done = f32[16,8192]{1,0:T(8,128)} async-done(((f32[64,8192]{1,0:T(8,128)}), f32[16,8192]{1,0:T(8,128)}) %reduce-scatter.5.cloned.1.call-update) | async-done | bytes 524304 | tf_op jit(solution)/shard_map/reduce_scatter | solution.py:30
  171.9 0.0 all-reduce.4.cloned.1.call-update
  171.9 0.0 copy-done.8
  172.0 0.6 dynamic-slice
  173.2 57.2 %all-reduce.4.cloned.1.call-done = f32[16,8192]{1,0:T(8,128)} async-done(((f32[16,8192]{1,0:T(8,128)}), f32[16,8192]{1,0:T(8,128)}) %all-reduce.4.cloned.1.call-update) | async-done | bytes 524304
  230.4 1.8 multiply_reduce_fusion
  232.2 0.5 broadcast_multiply_fusion
  (1 shorter events, 0.0 us)
Async XLA Ops:
  7.2 0.8 copy-start
  7.2 45.2 %copy-start.3 = (bf16[16,8192]{1,0:T(8,128)(2,1)S(1)}, bf16[16,8192]{1,0:T(8,128)(2,1)}, u32[]{:S(2)}) copy-start(bf16[16,8192]{1,0:T(8,128)(2,1)} %param.10) | copy-start | bytes 786436
  7.2 46.3 %copy-start.7 = (s32[64]{0:T(128)S(1)}, s32[64]{0:T(128)}, u32[]{:S(2)}) copy-start(s32[64]{0:T(128)} %param.11) | copy-start | bytes 772
  7.2 108.9 %copy-start.6 = (f32[1024]{0:T(1024)S(1)}, f32[1024]{0:T(1024)}, u32[]{:S(2)}) copy-start(f32[1024]{0:T(1024)} %param.13) | copy-start | bytes 12292
  7.2 108.9 %copy-start.5 = (f32[1024]{0:T(1024)S(1)}, f32[1024]{0:T(1024)}, u32[]{:S(2)}) copy-start(f32[1024]{0:T(1024)} %param.14) | copy-start | bytes 12292
  7.2 108.9 %copy-start.4 = (f32[8192]{0:T(1024)S(1)}, f32[8192]{0:T(1024)}, u32[]{:S(2)}) copy-start(f32[8192]{0:T(1024)} %param.15) | copy-start | bytes 98308
  7.2 45.1 %reduce-scatter.3.cloned.1.call-start = ((), (), s32[]{:S(2)}) async-start(), calls=%async_computation.2 | async-start | bytes 2621440 | tf_op jit(solution)/shard_map/reduce_scatter | solution.py:14
  14.3 157.6 %reduce-scatter.5.cloned.1.call-start = ((), (), s32[]{:S(2)}) async-start(), calls=%async_computation.3 | async-start | bytes 2621440 | tf_op jit(solution)/shard_map/reduce_scatter | solution.py:30
  53.5 71.5 %copy-start.1 = (bf16[16,8192]{1,0:T(8,128)(2,1)}, bf16[16,8192]{1,0:T(8,128)(2,1)S(1)}, u32[]{:S(2)}) copy-start(bf16[16,8192]{1,0:T(8,128)(2,1)S(1)} %add_convert_fusion) | copy-start | bytes 786436
  125.0 12.4 %copy-start.2 = (bf16[64,1024]{1,0:T(8,128)(2,1)}, bf16[64,1024]{1,0:T(8,128)(2,1)S(1)}, u32[]{:S(2)}) copy-start(bf16[64,1024]{1,0:T(8,128)(2,1)S(1)} %fusion.2) | copy-start | bytes 393220
  125.0 47.0 %copy-start.8 = (u32[32]{0:T(128)S(1)}, u32[32]{0:T(128)}, u32[]{:S(2)}) copy-start(u32[32]{0:T(128)} %constant.29) | copy-start | bytes 388
  137.4 93.0 %all-reduce.4.cloned.1.call-start = ((), (), s32[]{:S(2)}) async-start(), calls=%async_computation.4 | async-start | bytes 1048576
Sparse Core Ops, SparseCore 0:
  14.4 37.8 reduce-scatter.2
  137.5 34.3 reduce-scatter.4
  174.2 56.1 all-reduce.3
where the time goes:
time: 240 us; the launch traced here: 239 us
  waiting for transfers between devices  130 us (54%)
  blocking collectives  62.2 us (26%)
  matrix products  27.9 us (12%)
  between operations  14.6 us (6%)
  other arithmetic  3.38 us (1%)
    psum x1, blocking collectives, shards(): picked = lax.psum(owned, ('tp', 'lat')).astype(jnp.bfloat16)  62.2 us
    unnamed x4, waiting for transfers between devices  57.3 us
    reduce_scatter x1, waiting for transfers between devices, shards(): lax.psum_scatter(jnp.dot(block, w_out, preferred_element_type=jnp.float32...  38 us
    reduce_scatter x1, waiting for transfers between devices, shards(): lax.psum_scatter(lax.dot_general(block, w_enc, (((1,), (1,)), ((), ())),...  34.5 us
    dot_general x1, matrix products, shards(): lax.dot_general(block, w_enc, (((1,), (1,)), ((), ())), preferred_element...  12.3 us
    dot_general x1, matrix products, shards(): pre = jnp.dot(centered, w_enc, preferred_element_type=jnp.float32) + b_enc  8.8 us
    dot_general x1, matrix products, shards(): jnp.dot(block, w_out, preferred_element_type=jnp.float32)  6.28 us
  transfers between devices with their start and end apart: 3, of which 3 were waited for; matrix products, arithmetic and copies ran while one was open for 0% of the time, Pallas kernels for 0%

commit v1 on v0

v1 whole, which is shorter than its diff:
```python
import functools

import jax
import jax.numpy as jnp
from jax import lax
from jax.experimental import pallas as pl
from jax.experimental.pallas import tpu as pltpu
from jax.sharding import PartitionSpec as P

GROUPS = 4
LANES = 128
F32 = jnp.float32
BF16 = jnp.bfloat16
MESH = pl.DeviceIdType.MESH


def log2(n):
    return n.bit_length() - 1


def orders(n_tp, n_lat):
    tp_bits = [("tp", b) for b in range(log2(n_tp))]
    lat_bits = [("lat", b) for b in range(log2(n_lat))]
    out = []
    for g in range(GROUPS):
        turn = g % max(len(tp_bits), 1)
        out.append(lat_bits[:1] + tp_bits[turn:] + tp_bits[:turn] + lat_bits[1:])
    return out


def kernel(n_tp, n_lat, pos_ref, attn_ref, resid_ref, b_enc_ref, norm_ref, bdec_ref, w_out_hbm, w_enc_hbm,
           stream_ref, codes_ref, recon_ref, err_ref,
           w_out, w_enc, lhs, pick_own, acc, pk, snd, rcv_a, rcv_c, mix_snd, mix_rcv, mix_own, pre, cperm, mine,
           in_sem, enc_sem, a_send, a_recv, g_send, g_recv, c_send, c_recv, m_send, m_recv):
    ids = {"tp": lax.axis_index("tp"), "lat": lax.axis_index("lat")}
    n_dev = n_tp * n_lat
    rows, depth = attn_ref.shape
    own_rows, width = resid_ref.shape
    sel = pos_ref.shape[1]
    cg = width // LANES // GROUPS
    rg = cg * sel
    order = orders(n_tp, n_lat)
    n_steps = len(order[0])
    bit = lambda ab: lax.rem(lax.div(ids[ab[0]], 1 << ab[1]), 2)
    flip = lambda ab: {ab[0]: ids[ab[0]] + (1 - 2 * bit(ab)) * (1 << ab[1])}
    core = bit(order[0][0])
    half_cols = cg * LANES // 2

    def piece(g, which):
        h = 1 - core if which == 0 else core
        return pl.multiple_of(g * cg * LANES + h * half_cols, half_cols)

    loads = []
    for which in range(2):
        for g in range(GROUPS):
            cols = pl.ds(piece(g, which), half_cols)
            loads.append(pltpu.make_async_copy(w_out_hbm.at[:, cols], w_out.at[:, cols], in_sem.at[which * GROUPS + g]))
    n_enc = enc_sem.shape[0]
    enc_rows = width // n_enc
    enc_loads = [
        pltpu.make_async_copy(w_enc_hbm.at[pl.ds(i * enc_rows, enc_rows), :], w_enc.at[pl.ds(i * enc_rows, enc_rows), :], enc_sem.at[i])
        for i in range(n_enc)
    ]
    for load in loads + enc_loads:
        load.start()

    barrier = pltpu.get_barrier_semaphore()
    peers = [flip(("lat", b)) for b in range(log2(n_lat))]
    mix_peer = lambda d: lax.rem(ids["tp"] + d, n_tp)
    peers += [{"tp": mix_peer(d)} for d in range(1, n_tp)]
    for peer in peers:
        pl.semaphore_signal(barrier, inc=1, device_id=peer, device_id_type=MESH)

    base = ids["lat"] * rows
    hot = (lax.broadcasted_iota(jnp.int32, (rows, sel), 0) + base == pos_ref[...]).astype(BF16)
    lhs[0:rows, :] = attn_ref[...]
    lhs[rows:rows + sel, :] = lax.dot_general(hot, attn_ref[...], (((0,), (0,)), ((), ())), preferred_element_type=F32).astype(BF16)
    lhs[rows + sel:rows + sel + own_rows, :] = attn_ref[pl.ds(pl.multiple_of(ids["tp"] * own_rows, own_rows), own_rows), :]
    base = (ids["lat"] * n_tp + ids["tp"]) * own_rows
    hot = (lax.broadcasted_iota(jnp.int32, (own_rows, sel), 0) + base == pos_ref[...]).astype(BF16)
    eye = (lax.broadcasted_iota(jnp.int32, (own_rows, own_rows), 0) == lax.broadcasted_iota(jnp.int32, (own_rows, own_rows), 1)).astype(BF16)
    pick_own[...] = lax.dot_general(hot, eye, (((0,), (0,)), ((), ())), preferred_element_type=F32).astype(BF16)

    def halves(s):
        return rg - (rg >> s), rg >> (s + 1)

    def exchange(rcv, send_sem, recv_sem, g, s):
        off, size = halves(s)
        return pltpu.make_async_remote_copy(
            src_ref=snd.at[g, pl.ds(off, size), :],
            dst_ref=rcv.at[g, pl.ds(off, size), :],
            send_sem=send_sem.at[g * n_steps + s],
            recv_sem=recv_sem.at[g * n_steps + s],
            device_id=flip(order[g][s]),
            device_id_type=MESH,
        )

    tile = min(512, half_cols)
    per = tile // LANES
    for which in range(2):
        for g in range(GROUPS):
            loads[which * GROUPS + g].wait()
            first = piece(g, which)

            def body(i, _, which=which, g=g, first=first):
                cols = pl.ds(pl.multiple_of(first + i * tile, tile), tile)
                out = jnp.dot(lhs[...], w_out[:, cols], preferred_element_type=F32)
                mix_snd[:, cols] = out[0:rows].astype(BF16)
                mix_own[:, cols] = out[rows + sel:]
                part = out[rows:rows + sel] + jnp.dot(pick_own[...], resid_ref[:, cols], preferred_element_type=F32)
                for k in range(per):
                    block = part[:, k * LANES:(k + 1) * LANES]
                    at = (i * per + k) * sel
                    if which == 0:
                        snd[g, pl.ds(pl.multiple_of(at, sel), sel), :] = block.astype(BF16)
                    else:
                        acc[pl.ds(pl.multiple_of(g * rg + core * (rg // 2) + at, sel), sel), :] = block
                return 0

            lax.fori_loop(0, half_cols // tile, body, 0)
            if which == 0:
                if g == 0:
                    pl.semaphore_wait(barrier, len(peers))
                exchange(rcv_a, a_send, a_recv, g, 0).start()

    def starts(g):
        out = [0]
        for s in range(n_steps):
            out.append(out[-1] + bit(order[g][s]) * (rg >> (s + 1)))
        return out

    start = [starts(g) for g in range(GROUPS)]

    def span(at, size):
        return pl.ds(pl.multiple_of(at, size), size)

    def reduce(rcv, send_sem, recv_sem, last, between=None):
        for s in range(n_steps):
            off, size = halves(s)
            for g in range(GROUPS):
                exchange(rcv, send_sem, recv_sem, g, s).wait_recv()
                here = start[g][s + 1]
                if s + 1 < n_steps:
                    half = size // 2
                    b = bit(order[g][s + 1])
                    gone, kept = (1 - b) * half, b * half
                    to = halves(s + 1)[0]
                    snd[g, pl.ds(to, half), :] = (
                        acc[span(g * rg + here + gone, half), :] + rcv[g, span(off + gone, half), :].astype(F32)
                    ).astype(BF16)
                    exchange(rcv, send_sem, recv_sem, g, s + 1).start()
                    at = span(g * rg + here + kept, half)
                    acc[at, :] = acc[at, :] + rcv[g, span(off + kept, half), :].astype(F32)
                else:
                    last(g, here, size, acc[span(g * rg + here, size), :] + rcv[g, pl.ds(off, size), :].astype(F32))
            if s == 0 and between is not None:
                between()
        for s in range(n_steps):
            for g in range(GROUPS):
                exchange(rcv, send_sem, recv_sem, g, s).wait_send()

    def own_rows_done(g, here, size, total):
        pk[span(g * rg + here, size), :] = total.astype(BF16)

    reduce(rcv_a, a_send, a_recv, own_rows_done)

    def share(g, s):
        at = span(g * rg + start[g][s + 1], rg >> (s + 1))
        return pltpu.make_async_remote_copy(
            src_ref=pk.at[at, :],
            dst_ref=pk.at[at, :],
            send_sem=g_send.at[g * n_steps + s],
            recv_sem=g_recv.at[g * n_steps + s],
            device_id=flip(order[g][s]),
            device_id_type=MESH,
        )

    pre[...] = jnp.zeros_like(pre)
    n_tile = min(256, pre.shape[1])

    def encode(g, at, size):
        count = size // sel
        first = g * cg + lax.div(at, sel)
        parts = []
        for k in range(count):
            ct = first + k
            block = pk[pl.ds(pl.multiple_of(ct * sel, sel), sel), :].astype(F32)
            acc[pl.ds(pl.multiple_of(ct * sel, sel), sel), :] = block
            parts.append((block - bdec_ref[pl.ds(ct, 1), :]).astype(BF16))
        left = jnp.concatenate(parts, axis=1)
        deep = pl.ds(pl.multiple_of(first * LANES, count * LANES), count * LANES)

        def body(i, _):
            cols = pl.ds(pl.multiple_of(i * n_tile, n_tile), n_tile)
            pre[:, cols] += jnp.dot(left, w_enc[deep, cols], preferred_element_type=F32)
            return 0

        lax.fori_loop(0, pre.shape[1] // n_tile, body, 0)

    for s in reversed(range(n_steps)):
        for g in range(GROUPS):
            share(g, s).start()
        if s == 1:
            for load in enc_loads:
                load.wait()
        if s <= 1:
            for g in range(GROUPS):
                size = rg >> (s + 1)
                if s == 1:
                    encode(g, start[g][2], size)
                else:
                    encode(g, start[g][1] + (1 - bit(order[g][1])) * (rg >> 2), rg >> 2)
        for g in range(GROUPS):
            share(g, s).wait_recv()

    def mix(d):
        to = mix_peer(d)
        return pltpu.make_async_remote_copy(
            src_ref=mix_snd.at[pl.ds(pl.multiple_of(to * own_rows, own_rows), own_rows), :],
            dst_ref=mix_rcv.at[d - 1],
            send_sem=m_send.at[d - 1],
            recv_sem=m_recv.at[d - 1],
            device_id={"tp": to},
            device_id_type=MESH,
        )

    for d in range(1, n_tp):
        mix(d).start()
    for g in range(GROUPS):
        encode(g, (1 - core) * (rg // 2), rg // 2)
    for s in range(n_steps):
        for g in range(GROUPS):
            share(g, s).wait_send()

    codes = (jnp.maximum(pre[...] + b_enc_ref[...], 0.0) * norm_ref[...]).astype(BF16)
    codes_ref[...] = codes

    keep = sel // n_dev
    me = ids["tp"] * n_lat + ids["lat"]
    for r in range(keep):
        mine[r] = acc[pl.ds(me * keep + r, width // LANES, stride=sel), :]

    kinds = {}
    for g in range(GROUPS):
        if tuple(order[g]) not in kinds:
            q = lax.broadcasted_iota(jnp.int32, (sel, sel), 0)
            chunk = lax.div(q, keep)
            row = lax.rem(q, keep)
            for i, (axis, b) in enumerate(order[g]):
                weight = keep * (1 << b) * (n_lat if axis == "tp" else 1)
                row = row + lax.rem(lax.div(chunk, 1 << (n_steps - 1 - i)), 2) * weight
            turn = (row == lax.broadcasted_iota(jnp.int32, (sel, sel), 1)).astype(BF16)
            kinds[tuple(order[g])] = len(kinds)
            cperm[len(kinds) - 1] = jnp.dot(turn, codes, preferred_element_type=F32).astype(BF16)
    d_tile = min(256, cg * LANES)
    d_per = d_tile // LANES
    for g in range(GROUPS):
        left = cperm[kinds[tuple(order[g])]]

        def body(i, _, g=g, left=left):
            at = pl.ds(pl.multiple_of(g * cg * LANES + i * d_tile, d_tile), d_tile)
            out = lax.dot_general(left, w_enc[at, :], (((1,), (1,)), ((), ())), preferred_element_type=F32)
            for k in range(d_per):
                acc[pl.ds(g * rg + i * d_per + k, sel, stride=cg), :] = out[:, k * LANES:(k + 1) * LANES]
            return 0

        lax.fori_loop(0, cg * LANES // d_tile, body, 0)
        half = rg // 2
        snd[g, pl.ds(0, half), :] = acc[span(g * rg + (1 - core) * half, half), :].astype(BF16)
        exchange(rcv_c, c_send, c_recv, g, 0).start()

    sums = [None] * keep

    def score(g, here, size, total):
        for r in range(keep):
            full = total[r * cg:(r + 1) * cg] + bdec_ref[g * cg:(g + 1) * cg, :]
            recon_ref[r * (width // LANES) + g * cg:r * (width // LANES) + (g + 1) * cg, :] = full.astype(BF16)
            off = full - mine[r, g * cg:(g + 1) * cg, :]
            sums[r] = off * off if sums[r] is None else sums[r] + off * off

    def keep_stream():
        for d in range(1, n_tp):
            mix(d).wait_recv()

        def body(i, _):
            cols = pl.ds(pl.multiple_of(i * 1024, 1024), 1024)
            total = mix_own[:, cols]
            for d in range(1, n_tp):
                total = total + mix_rcv[d - 1, :, cols].astype(F32)
            stream_ref[:, cols] = (resid_ref[:, cols].astype(F32) + total).astype(BF16)
            return 0

        lax.fori_loop(0, width // 1024, body, 0)

    reduce(rcv_c, c_send, c_recv, score, keep_stream)
    for r in range(keep):
        total = jnp.sum(jnp.sum(sums[r], axis=0, keepdims=True), axis=1, keepdims=True) / width
        err_ref[r:r + 1, :] = jnp.broadcast_to(total, (1, LANES))
    for d in range(1, n_tp):
        mix(d).wait_send()


def shards(attn_out, w_out, resid_in, positions, w_enc, b_enc, dec_norm, b_dec):
    n_tp = lax.axis_size("tp")
    n_lat = lax.axis_size("lat")
    n_dev = n_tp * n_lat
    rows, depth = attn_out.shape
    own_rows, width = resid_in.shape
    sel = positions.shape[0]
    lats = w_enc.shape[1]
    keep = sel // n_dev
    feats = width // LANES
    rg = feats // GROUPS * sel
    n_steps = log2(n_dev)
    vmem = pl.BlockSpec(memory_space=pltpu.VMEM)
    hbm = pl.BlockSpec(memory_space=pl.ANY)
    dma = pltpu.SemaphoreType.DMA
    n_sem = GROUPS * n_steps
    stream, codes, recon, err = pl.pallas_call(
        functools.partial(kernel, n_tp, n_lat),
        out_shape=(
            jax.ShapeDtypeStruct((own_rows, width), BF16),
            jax.ShapeDtypeStruct((sel, lats), BF16),
            jax.ShapeDtypeStruct((keep * feats, LANES), BF16),
            jax.ShapeDtypeStruct((keep, LANES), F32),
        ),
        in_specs=[vmem] * 6 + [hbm] * 2,
        out_specs=(vmem,) * 4,
        scratch_shapes=[
            pltpu.VMEM((depth, width), BF16),
            pltpu.VMEM((width, lats), BF16),
            pltpu.VMEM((rows + sel + own_rows, depth), BF16),
            pltpu.VMEM((sel, own_rows), BF16),
            pltpu.VMEM((GROUPS * rg, LANES), F32),
            pltpu.VMEM((GROUPS * rg, LANES), BF16),
            pltpu.VMEM((GROUPS, rg, LANES), BF16),
            pltpu.VMEM((GROUPS, rg, LANES), BF16),
            pltpu.VMEM((GROUPS, rg, LANES), BF16),
            pltpu.VMEM((rows, width), BF16),
            pltpu.VMEM((n_tp - 1, own_rows, width), BF16),
            pltpu.VMEM((own_rows, width), F32),
            pltpu.VMEM((sel, lats), F32),
            pltpu.VMEM((min(GROUPS, log2(n_tp)), sel, lats), BF16),
            pltpu.VMEM((keep, feats, LANES), F32),
            dma((2 * GROUPS,)),
            dma((8,)),
            dma((n_sem,)), dma((n_sem,)),
            dma((n_sem,)), dma((n_sem,)),
            dma((n_sem,)), dma((n_sem,)),
            dma((n_tp - 1,)), dma((n_tp - 1,)),
        ],
        compiler_params=pltpu.CompilerParams(
            collective_id=0, has_side_effects=True, vmem_limit_bytes=60 * 1024 * 1024
        ),
        cost_estimate=pl.CostEstimate(
            flops=2 * (2 * sel * width * lats + (rows + sel + own_rows) * depth * width),
            bytes_accessed=2 * (w_out.size + w_enc.size),
            transcendentals=0,
        ),
    )(
        positions.reshape(1, sel),
        attn_out,
        resid_in,
        b_enc.reshape(1, lats),
        dec_norm.reshape(1, lats),
        b_dec.reshape(feats, LANES),
        w_out,
        w_enc,
    )
    return stream, codes, recon.reshape(keep, width), err[:, 0]


def solution(mesh):
    placed = (
        P("lat", "tp"),
        P("tp", None),
        P(("lat", "tp"), None),
        P(),
        P(None, ("tp", "lat")),
        P(("tp", "lat")),
        P(("tp", "lat")),
        P(),
    )
    return jax.shard_map(
        shards,
        mesh=mesh,
        in_specs=placed,
        out_specs=(
            P(("lat", "tp"), None),
            P(None, ("tp", "lat")),
            P(("tp", "lat"), None),
            P(("tp", "lat")),
        ),
        check_vma=False,
    )
```

time: 240 us -> 79.7 us (0.33)
  waiting for transfers between devices: 130 us -> 0 us
  Pallas kernels: 0 us -> 72.8 us
  blocking collectives: 62.2 us -> 0 us
  matrix products: 27.9 us -> 0 us
  between operations: 14.6 us -> 0.64 us
  local copies, waits for them, and re-layouts: 1.37 us -> 5.93 us
  other arithmetic: 3.38 us -> 0 us
    pallas_call x0 -> x1, Pallas kernels: none -> 72.8 us  [shards(): pl.pallas_call(functools.partial(kernel, n_tp, n_lat), out_shape=(jax.Sha...]
    reduce_scatter x2 -> x0, waiting for transfers between devices: 72.5 us -> none  [the longest x1 38 us: shards(): lax.psum_scatter(jnp.dot(block, w_out, preferred_element_type=jnp.float32...]
    psum x1 -> x0, blocking collectives: 62.2 us -> none  [shards(): picked = lax.psum(owned, ('tp', 'lat')).astype(jnp.bfloat16)]
    unnamed x4 -> x0, waiting for transfers between devices: 57.3 us -> none
    dot_general x4 -> x0, matrix products: 27.9 us -> none  [the longest x1 12.3 us: shards(): lax.dot_general(block, w_enc, (((1,), (1,)), ((), ())), preferred_element...]
  transfers between devices with their start and end apart: 3 -> 0, of which waited for: 3 -> 0; matrix products, arithmetic and copies ran while one was open for 0% -> 0% of each run, Pallas kernels for 0% -> 0%
where the time goes in v1:
time: 79.7 us; the launch traced here: 79.4 us
  Pallas kernels  72.8 us (91%)
  local copies, waits for them, and re-layouts  5.93 us (7%)
    pallas_call x1, Pallas kernels, shards(): pl.pallas_call(functools.partial(kernel, n_tp, n_lat), out_shape=(jax.Sha...  72.8 us
    unnamed x2, local copies, waits for them, and re-layouts  3.24 us

profile of v1, /device:TPU:0, one launch (start us, length us, event | category | flops | bytes accessed | tf_op | source)
XLA Modules:
  0.0 79.4 jit_solution(12838327636508656819)
XLA Ops:
  0.6 72.8 %shard_map.111 = (bf16[16,8192]{1,0:T(8,128)(2,1)}, bf16[64,1024]{1,0:T(8,128)(2,1)}, bf16[128,128]{1,0:T(8,128)(2,1)}, f32[2,128]{1,0:T(2,128)}) custom-call(s32[1,64]{1,0:T(1,128)} %bitcast.7, bf16[64,512]{1,0:T(8,128)(2,1)} %attn_ref.1, bf16[16,8192]{1,0:T(8,128)(2,1)} %resid_ref.1, f32[1,1024]{1,0:T(1,128)} %bitcast.5, f32[1,1024]{1,0:T(1,128)} %bitcast.6, ...), custom_call_target="tpu_custom_call" | custom-call | flops 3355443200 | bytes 25165824 | tf_op jit(solution)/shard_map/pallas_call | solution.py:319
  73.5 1.3 %slice_reduce_fusion = f32[2]{0:T(128)} fusion(f32[2,128]{1,0:T(2,128)} %get-tuple-element.11), kind=kLoop, calls=%fused_computation | loop fusion | bytes 16 | tf_op jit(solution)/shard_map/slice | solution.py:370
  74.8 1.4 %reshape.27 = bf16[2,8192]{1,0:T(2,128)(2,1)} reshape(bf16[128,128]{1,0:T(8,128)(2,1)} %get-tuple-element.10) | data formatting | bytes 65536 | tf_op jit(solution)/shard_map/reshape | solution.py:370
  76.2 1.7 %copy.14 = bf16[16,8192]{1,0:T(8,128)(2,1)} copy(bf16[16,8192]{1,0:T(8,128)(2,1)} %get-tuple-element.16) | data formatting | bytes 524288
  77.8 1.6 %copy.15 = bf16[64,1024]{1,0:T(8,128)(2,1)} copy(bf16[64,1024]{1,0:T(8,128)(2,1)} %get-tuple-element.17) | data formatting | bytes 262144

commit v2 on v1

v2 whole, which is shorter than its diff:
```python
import functools

import jax
import jax.numpy as jnp
from jax import lax
from jax.experimental import pallas as pl
from jax.experimental.pallas import tpu as pltpu
from jax.sharding import PartitionSpec as P

GROUPS = 4
LANES = 128
F32 = jnp.float32
BF16 = jnp.bfloat16
MESH = pl.DeviceIdType.MESH


def log2(n):
    return n.bit_length() - 1


def digits(n_tp, n_lat):
    tp_bits, lat_bits = log2(n_tp), log2(n_lat)
    out = [("lat", 0, 2)] if lat_bits else []
    out += [("tp", b, 1 << min(2, tp_bits - b)) for b in range(0, tp_bits, 2)]
    out += [("lat", b, 1 << min(2, lat_bits - b)) for b in range(1, lat_bits, 2)]
    return out


def kernel(n_tp, n_lat, pos_ref, attn_ref, resid_ref, b_enc_ref, norm_ref, bdec_ref, w_out_hbm, w_enc_hbm,
           stream_ref, codes_ref, recon_ref, err_ref,
           w_out, w_enc, lhs, pick_own, acc, pk, snd, rcv_a, rcv_c, mix_snd, mix_rcv, mix_own, pre, cperm, mine,
           in_sem, enc_sem, a_send, a_recv, g_send, g_recv, c_send, c_recv, m_send, m_recv):
    ids = {"tp": lax.axis_index("tp"), "lat": lax.axis_index("lat")}
    n_dev = n_tp * n_lat
    rows, depth = attn_ref.shape
    own_rows, width = resid_ref.shape
    sel = pos_ref.shape[1]
    cg = width // LANES // GROUPS
    rg = cg * sel
    steps = digits(n_tp, n_lat)
    n_steps = len(steps)
    digit = [lax.rem(lax.div(ids[axis], 1 << low), radix) for axis, low, radix in steps]
    sizes = [rg]
    for axis, low, radix in steps:
        sizes.append(sizes[-1] // radix)
    offs = [0]
    sem_at = [0]
    for s in range(n_steps):
        offs.append(offs[-1] + (steps[s][2] - 1) * sizes[s + 1])
        sem_at.append(sem_at[-1] + steps[s][2] - 1)
    start = [0]
    for s in range(n_steps):
        start.append(start[-1] + digit[s] * sizes[s + 1])

    def towards(s, d):
        return lax.rem(digit[s] + d, steps[s][2])

    def peer(s, d):
        axis, low, radix = steps[s]
        return {axis: ids[axis] + (towards(s, d) - digit[s]) * (1 << low)}

    core = digit[0]
    half_cols = cg * LANES // 2

    def piece(g, which):
        h = 1 - core if which == 0 else core
        return pl.multiple_of(g * cg * LANES + h * half_cols, half_cols)

    def load(g, which):
        cols = pl.ds(piece(g, which), half_cols)
        return pltpu.make_async_copy(w_out_hbm.at[:, cols], w_out.at[:, cols], in_sem.at[which * GROUPS + g])

    load(0, 0).start()
    for g in range(GROUPS):
        if g + 1 < GROUPS:
            load(g + 1, 0).start()
        load(g, 1).start()
    n_enc = enc_sem.shape[0]
    enc_rows = width // n_enc
    enc_loads = [
        pltpu.make_async_copy(w_enc_hbm.at[pl.ds(i * enc_rows, enc_rows), :], w_enc.at[pl.ds(i * enc_rows, enc_rows), :], enc_sem.at[i])
        for i in range(n_enc)
    ]
    for one in enc_loads:
        one.start()

    barrier = pltpu.get_barrier_semaphore()
    mix_peer = lambda d: lax.rem(ids["tp"] + d, n_tp)
    peers = [peer(s, d) for s in range(n_steps) if steps[s][0] == "lat" for d in range(1, steps[s][2])]
    peers += [{"tp": mix_peer(d)} for d in range(1, n_tp)]
    for one in peers:
        pl.semaphore_signal(barrier, inc=1, device_id=one, device_id_type=MESH)

    base = ids["lat"] * rows
    hot = (lax.broadcasted_iota(jnp.int32, (rows, sel), 0) + base == pos_ref[...]).astype(BF16)
    lhs[0:rows, :] = attn_ref[...]
    lhs[rows:rows + sel, :] = lax.dot_general(hot, attn_ref[...], (((0,), (0,)), ((), ())), preferred_element_type=F32).astype(BF16)
    lhs[rows + sel:rows + sel + own_rows, :] = attn_ref[pl.ds(pl.multiple_of(ids["tp"] * own_rows, own_rows), own_rows), :]
    base = (ids["lat"] * n_tp + ids["tp"]) * own_rows
    hot = (lax.broadcasted_iota(jnp.int32, (own_rows, sel), 0) + base == pos_ref[...]).astype(BF16)
    eye = (lax.broadcasted_iota(jnp.int32, (own_rows, own_rows), 0) == lax.broadcasted_iota(jnp.int32, (own_rows, own_rows), 1)).astype(BF16)
    pick_own[...] = lax.dot_general(hot, eye, (((0,), (0,)), ((), ())), preferred_element_type=F32).astype(BF16)

    def span(at, size):
        return pl.ds(pl.multiple_of(at, size), size)

    def exchange(rcv, send_sem, recv_sem, g, s, d):
        at = pl.ds(offs[s] + (d - 1) * sizes[s + 1], sizes[s + 1])
        sem = g * sem_at[-1] + sem_at[s] + d - 1
        return pltpu.make_async_remote_copy(
            src_ref=snd.at[g, at, :],
            dst_ref=rcv.at[g, at, :],
            send_sem=send_sem.at[sem],
            recv_sem=recv_sem.at[sem],
            device_id=peer(s, d),
            device_id_type=MESH,
        )

    tile = min(512, half_cols)
    per = tile // LANES

    def project(g, which):
        load(g, which).wait()
        first = piece(g, which)

        def body(i, _):
            cols = pl.ds(pl.multiple_of(first + i * tile, tile), tile)
            out = jnp.dot(lhs[...], w_out[:, cols], preferred_element_type=F32)
            mix_snd[:, cols] = out[0:rows].astype(BF16)
            mix_own[:, cols] = out[rows + sel:]
            part = out[rows:rows + sel] + jnp.dot(pick_own[...], resid_ref[:, cols], preferred_element_type=F32)
            for k in range(per):
                block = part[:, k * LANES:(k + 1) * LANES]
                at = (i * per + k) * sel
                if which == 0:
                    snd[g, pl.ds(pl.multiple_of(at, sel), sel), :] = block.astype(BF16)
                else:
                    acc[pl.ds(pl.multiple_of(g * rg + core * (rg // 2) + at, sel), sel), :] = block
            return 0

        lax.fori_loop(0, half_cols // tile, body, 0)
        if which == 0:
            if g == 0:
                pl.semaphore_wait(barrier, len(peers))
            exchange(rcv_a, a_send, a_recv, g, 0, 1).start()

    def take(rcv, send_sem, recv_sem, last, g, s):
        radix = steps[s][2]
        for d in range(1, radix):
            exchange(rcv, send_sem, recv_sem, g, s, d).wait_recv()

        def total(at, size):
            out = acc[span(g * rg + start[s + 1] + at, size), :]
            for d in range(1, radix):
                out = out + rcv[g, span(offs[s] + (d - 1) * sizes[s + 1] + at, size), :].astype(F32)
            return out

        if s + 1 == n_steps:
            last(g, total(0, sizes[s + 1]))
            return
        size = sizes[s + 2]
        for d in range(1, steps[s + 1][2]):
            snd[g, pl.ds(offs[s + 1] + (d - 1) * size, size), :] = total(towards(s + 1, d) * size, size).astype(BF16)
            exchange(rcv, send_sem, recv_sem, g, s + 1, d).start()
        acc[span(g * rg + start[s + 2], size), :] = total(digit[s + 1] * size, size)

    def sent(rcv, send_sem, recv_sem):
        for g in range(GROUPS):
            for s in range(n_steps):
                for d in range(1, steps[s][2]):
                    exchange(rcv, send_sem, recv_sem, g, s, d).wait_send()

    def share(g, s, d):
        at = span(g * rg + start[s + 1], sizes[s + 1])
        sem = g * sem_at[-1] + sem_at[s] + d - 1
        return pltpu.make_async_remote_copy(
            src_ref=pk.at[at, :],
            dst_ref=pk.at[at, :],
            send_sem=g_send.at[sem],
            recv_sem=g_recv.at[sem],
            device_id=peer(s, d),
            device_id_type=MESH,
        )

    def share_start(g, s):
        for d in range(1, steps[s][2]):
            share(g, s, d).start()

    def share_take(g, s):
        for d in range(1, steps[s][2]):
            share(g, s, d).wait_recv()

    def own_rows_done(g, total):
        pk[span(g * rg + start[n_steps], sizes[n_steps]), :] = total.astype(BF16)
        share_start(g, n_steps - 1)

    n_tile = min(256, pre.shape[1])

    def encode(g, at, size):
        count = size // sel
        first = g * cg + lax.div(at, sel)
        parts = []
        for k in range(count):
            ct = first + k
            block = pk[pl.ds(pl.multiple_of(ct * sel, sel), sel), :].astype(F32)
            acc[pl.ds(pl.multiple_of(ct * sel, sel), sel), :] = block
            parts.append((block - bdec_ref[pl.ds(ct, 1), :]).astype(BF16))
        left = jnp.concatenate(parts, axis=1)
        deep = pl.ds(pl.multiple_of(first * LANES, count * LANES), count * LANES)

        def body(i, _):
            cols = pl.ds(pl.multiple_of(i * n_tile, n_tile), n_tile)
            pre[:, cols] += jnp.dot(left, w_enc[deep, cols], preferred_element_type=F32)
            return 0

        lax.fori_loop(0, pre.shape[1] // n_tile, body, 0)

    def mix(d):
        to = mix_peer(d)
        return pltpu.make_async_remote_copy(
            src_ref=mix_snd.at[pl.ds(pl.multiple_of(to * own_rows, own_rows), own_rows), :],
            dst_ref=mix_rcv.at[d - 1],
            send_sem=m_send.at[d - 1],
            recv_sem=m_recv.at[d - 1],
            device_id={"tp": to},
            device_id_type=MESH,
        )

    def wave(ops, after=None):
        for t in range(len(ops) + GROUPS - 1):
            for g in reversed(range(GROUPS)):
                if 0 <= t - g < len(ops):
                    ops[t - g](g)
            if after is not None:
                after(t)

    def encode_near(g):
        share_take(g, 1)
        share_start(g, 0)
        if g == GROUPS - 1:
            for d in range(1, n_tp):
                mix(d).start()
        if g == 0:
            for one in enc_loads:
                one.wait()
        encode(g, start[1], rg // 2)

    def encode_far(g):
        share_take(g, 0)
        encode(g, (1 - core) * (rg // 2), rg // 2)

    def pass_on(g, s):
        share_take(g, s)
        share_start(g, s - 1)

    pre[...] = jnp.zeros_like(pre)
    ops = [functools.partial(project, which=0), functools.partial(project, which=1)]
    ops += [functools.partial(take, rcv_a, a_send, a_recv, own_rows_done, s=s) for s in range(n_steps)]
    ops += [functools.partial(pass_on, s=s) for s in reversed(range(2, n_steps))]
    ops += [encode_near, encode_far]
    wave(ops)
    sent(rcv_a, a_send, a_recv)
    for g in range(GROUPS):
        for s in range(n_steps):
            for d in range(1, steps[s][2]):
                share(g, s, d).wait_send()

    codes = (jnp.maximum(pre[...] + b_enc_ref[...], 0.0) * norm_ref[...]).astype(BF16)
    codes_ref[...] = codes

    keep = sel // n_dev
    me = ids["tp"] * n_lat + ids["lat"]
    for r in range(keep):
        mine[r] = acc[pl.ds(me * keep + r, width // LANES, stride=sel), :]

    q = lax.broadcasted_iota(jnp.int32, (sel, sel), 0)
    row = lax.rem(q, keep)
    for s, (axis, low, radix) in enumerate(steps):
        weight = keep * (1 << low) * (n_lat if axis == "tp" else 1)
        row = row + lax.rem(lax.div(q, sizes[s + 1] // cg), radix) * weight
    turn = (row == lax.broadcasted_iota(jnp.int32, (sel, sel), 1)).astype(BF16)
    cperm[...] = jnp.dot(turn, codes, preferred_element_type=F32).astype(BF16)
    d_tile = min(256, cg * LANES)
    d_per = d_tile // LANES

    def decode(g):
        left = cperm[...]

        def body(i, _):
            at = pl.ds(pl.multiple_of(g * cg * LANES + i * d_tile, d_tile), d_tile)
            out = lax.dot_general(left, w_enc[at, :], (((1,), (1,)), ((), ())), preferred_element_type=F32)
            for k in range(d_per):
                acc[pl.ds(g * rg + i * d_per + k, sel, stride=cg), :] = out[:, k * LANES:(k + 1) * LANES]
            return 0

        lax.fori_loop(0, cg * LANES // d_tile, body, 0)
        half = rg // 2
        snd[g, pl.ds(0, half), :] = acc[span(g * rg + (1 - core) * half, half), :].astype(BF16)
        exchange(rcv_c, c_send, c_recv, g, 0, 1).start()

    sums = [None] * keep

    def score(g, total):
        for r in range(keep):
            full = total[r * cg:(r + 1) * cg] + bdec_ref[g * cg:(g + 1) * cg, :]
            recon_ref[r * (width // LANES) + g * cg:r * (width // LANES) + (g + 1) * cg, :] = full
            off = full - mine[r, g * cg:(g + 1) * cg, :]
            sums[r] = off * off if sums[r] is None else sums[r] + off * off

    def keep_stream(t):
        if t != GROUPS:
            return
        for d in range(1, n_tp):
            mix(d).wait_recv()

        def body(i, _):
            cols = pl.ds(pl.multiple_of(i * 1024, 1024), 1024)
            total = mix_own[:, cols]
            for d in range(1, n_tp):
                total = total + mix_rcv[d - 1, :, cols].astype(F32)
            stream_ref[:, cols] = (resid_ref[:, cols].astype(F32) + total).astype(BF16)
            return 0

        lax.fori_loop(0, width // 1024, body, 0)

    ops = [decode] + [functools.partial(take, rcv_c, c_send, c_recv, score, s=s) for s in range(n_steps)]
    wave(ops, keep_stream)
    for r in range(keep):
        total = jnp.sum(jnp.sum(sums[r], axis=0, keepdims=True), axis=1, keepdims=True) / width
        err_ref[r:r + 1, :] = jnp.broadcast_to(total, (1, LANES))
    sent(rcv_c, c_send, c_recv)
    for d in range(1, n_tp):
        mix(d).wait_send()


def finish(stream_in, codes_in, recon_in, err_in, stream_ref, codes_ref, recon_ref, err_ref):
    stream_ref[...] = stream_in[...]
    codes_ref[...] = codes_in[...]
    keep, width = recon_ref.shape
    feats = width // LANES
    for c in range(feats):
        recon_ref[:, c * LANES:(c + 1) * LANES] = recon_in[pl.ds(c, keep, stride=feats), :].astype(BF16)
    for r in range(keep):
        err_ref[r] = err_in[r, 0]


def shards(attn_out, w_out, resid_in, positions, w_enc, b_enc, dec_norm, b_dec):
    n_tp = lax.axis_size("tp")
    n_lat = lax.axis_size("lat")
    n_dev = n_tp * n_lat
    rows, depth = attn_out.shape
    own_rows, width = resid_in.shape
    sel = positions.shape[0]
    lats = w_enc.shape[1]
    keep = sel // n_dev
    feats = width // LANES
    rg = feats // GROUPS * sel
    n_sem = GROUPS * sum(radix - 1 for _, _, radix in digits(n_tp, n_lat))
    vmem = pl.BlockSpec(memory_space=pltpu.VMEM)
    hbm = pl.BlockSpec(memory_space=pl.ANY)
    dma = pltpu.SemaphoreType.DMA
    made = pl.pallas_call(
        functools.partial(kernel, n_tp, n_lat),
        out_shape=(
            jax.ShapeDtypeStruct((own_rows, width), BF16),
            jax.ShapeDtypeStruct((sel, lats), BF16),
            jax.ShapeDtypeStruct((keep * feats, LANES), F32),
            jax.ShapeDtypeStruct((keep, LANES), F32),
        ),
        in_specs=[vmem] * 6 + [hbm] * 2,
        out_specs=(vmem,) * 4,
        scratch_shapes=[
            pltpu.VMEM((depth, width), BF16),
            pltpu.VMEM((width, lats), BF16),
            pltpu.VMEM((rows + sel + own_rows, depth), BF16),
            pltpu.VMEM((sel, own_rows), BF16),
            pltpu.VMEM((GROUPS * rg, LANES), F32),
            pltpu.VMEM((GROUPS * rg, LANES), BF16),
            pltpu.VMEM((GROUPS, rg, LANES), BF16),
            pltpu.VMEM((GROUPS, rg, LANES), BF16),
            pltpu.VMEM((GROUPS, rg, LANES), BF16),
            pltpu.VMEM((rows, width), BF16),
            pltpu.VMEM((n_tp - 1, own_rows, width), BF16),
            pltpu.VMEM((own_rows, width), F32),
            pltpu.VMEM((sel, lats), F32),
            pltpu.VMEM((sel, lats), BF16),
            pltpu.VMEM((keep, feats, LANES), F32),
            dma((2 * GROUPS,)),
            dma((8,)),
            dma((n_sem,)), dma((n_sem,)),
            dma((n_sem,)), dma((n_sem,)),
            dma((n_sem,)), dma((n_sem,)),
            dma((n_tp - 1,)), dma((n_tp - 1,)),
        ],
        compiler_params=pltpu.CompilerParams(
            collective_id=0, has_side_effects=True, vmem_limit_bytes=60 * 1024 * 1024
        ),
        cost_estimate=pl.CostEstimate(
            flops=2 * (2 * sel * width * lats + (rows + sel + own_rows) * depth * width),
            bytes_accessed=2 * (w_out.size + w_enc.size),
            transcendentals=0,
        ),
    )(
        positions.reshape(1, sel),
        attn_out,
        resid_in,
        b_enc.reshape(1, lats),
        dec_norm.reshape(1, lats),
        b_dec.reshape(feats, LANES),
        w_out,
        w_enc,
    )
    smem = pl.BlockSpec(memory_space=pltpu.SMEM)
    return pl.pallas_call(
        finish,
        out_shape=(
            jax.ShapeDtypeStruct((own_rows, width), BF16),
            jax.ShapeDtypeStruct((sel, lats), BF16),
            jax.ShapeDtypeStruct((keep, width), BF16),
            jax.ShapeDtypeStruct((keep,), F32),
        ),
        in_specs=[vmem] * 3 + [smem],
        out_specs=(vmem,) * 3 + (smem,),
    )(*made)


def solution(mesh):
    placed = (
        P("lat", "tp"),
        P("tp", None),
        P(("lat", "tp"), None),
        P(),
        P(None, ("tp", "lat")),
        P(("tp", "lat")),
        P(("tp", "lat")),
        P(),
    )
    return jax.shard_map(
        shards,
        mesh=mesh,
        in_specs=placed,
        out_specs=(
            P(("lat", "tp"), None),
            P(None, ("tp", "lat")),
            P(("tp", "lat"), None),
            P(("tp", "lat")),
        ),
        check_vma=False,
    )
```

time: 79.7 us -> 62.9 us (0.79)
  Pallas kernels: 72.8 us -> 62.1 us
  local copies, waits for them, and re-layouts: 5.93 us -> 0 us
    pallas_call x1, Pallas kernels: 72.8 us -> 60.2 us  [shards(): pl.pallas_call(functools.partial(kernel, n_tp, n_lat), out_shape=(jax.Sha...]
    unnamed x2 -> x0, local copies, waits for them, and re-layouts: 3.24 us -> none
    pallas_call x0 -> x1, Pallas kernels: none -> 1.82 us  [shards(): pl.pallas_call(finish, out_shape=(jax.ShapeDtypeStruct((own_rows, width),...]
    reshape x1 -> x0, local copies, waits for them, and re-layouts: 1.38 us -> none  [shards(): return (stream, codes, recon.reshape(keep, width), err[:, 0])]
    slice x1 -> x0, local copies, waits for them, and re-layouts: 1.31 us -> none  [shards(): return (stream, codes, recon.reshape(keep, width), err[:, 0])]
where the time goes in v2:
time: 62.9 us; the launch traced here: 62.7 us
  Pallas kernels  62.1 us (99%)
  between operations  0.64 us (1%)
    pallas_call x1, Pallas kernels, shards(): pl.pallas_call(functools.partial(kernel, n_tp, n_lat), out_shape=(jax.Sha...  60.2 us
    pallas_call x1, Pallas kernels, shards(): pl.pallas_call(finish, out_shape=(jax.ShapeDtypeStruct((own_rows, width),...  1.82 us

profile of v2, /device:TPU:0, one launch (start us, length us, event | category | flops | bytes accessed | tf_op | source)
XLA Modules:
  0.0 62.7 jit_solution(4251421754672119608)
XLA Ops:
  0.6 60.2 %shard_map.111 = (bf16[16,8192]{1,0:T(8,128)(2,1)}, bf16[64,1024]{1,0:T(8,128)(2,1)}, f32[128,128]{1,0:T(8,128)}, f32[2,128]{1,0:T(2,128)}) custom-call(s32[1,64]{1,0:T(1,128)} %bitcast.7, bf16[64,512]{1,0:T(8,128)(2,1)} %attn_ref.1, bf16[16,8192]{1,0:T(8,128)(2,1)} %resid_ref.1, f32[1,1024]{1,0:T(1,128)} %bitcast.5, f32[1,1024]{1,0:T(1,128)} %bitcast.6, ...), custom_call_target="tpu_custom_call" | custom-call | flops 3355443200 | bytes 25165824 | tf_op jit(solution)/shard_map/pallas_call | solution.py:362
  60.9 1.8 %shard_map.112 = (bf16[16,8192]{1,0:T(8,128)(2,1)}, bf16[64,1024]{1,0:T(8,128)(2,1)}, bf16[2,8192]{1,0:T(2,128)(2,1)}, f32[2]{0:T(128)}) custom-call(bf16[16,8192]{1,0:T(8,128)(2,1)} %get-tuple-element.8.stream_in, bf16[64,1024]{1,0:T(8,128)(2,1)} %get-tuple-element.9.codes_in, f32[128,128]{1,0:T(8,128)} %get-tuple-element.10.recon_in, ...), custom_call_target="tpu_custom_call" | custom-call | tf_op jit(solution)/shard_map/pallas_call | solution.py:414

commit v3 on v2

--- a/solution.py
+++ b/solution.py
@@ -81,8 +81,6 @@
         pltpu.make_async_copy(w_enc_hbm.at[pl.ds(i * enc_rows, enc_rows), :], w_enc.at[pl.ds(i * enc_rows, enc_rows), :], enc_sem.at[i])
         for i in range(n_enc)
     ]
-    for one in enc_loads:
-        one.start()
 
     barrier = pltpu.get_barrier_semaphore()
     mix_peer = lambda d: lax.rem(ids["tp"] + d, n_tp)
@@ -121,6 +119,9 @@
 
     def project(g, which):
         load(g, which).wait()
+        if g == GROUPS - 1 and which == 0:
+            for one in enc_loads:
+                one.start()
         first = piece(g, which)
 
         def body(i, _):
@@ -138,7 +139,7 @@
                     acc[pl.ds(pl.multiple_of(g * rg + core * (rg // 2) + at, sel), sel), :] = block
             return 0
 
-        lax.fori_loop(0, half_cols // tile, body, 0)
+        lax.fori_loop(0, half_cols // tile, body, 0, unroll=True)
         if which == 0:
             if g == 0:
                 pl.semaphore_wait(barrier, len(peers))
@@ -213,7 +214,7 @@
             pre[:, cols] += jnp.dot(left, w_enc[deep, cols], preferred_element_type=F32)
             return 0
 
-        lax.fori_loop(0, pre.shape[1] // n_tile, body, 0)
+        lax.fori_loop(0, pre.shape[1] // n_tile, body, 0, unroll=True)
 
     def mix(d):
         to = mix_peer(d)
@@ -293,7 +294,7 @@
                 acc[pl.ds(g * rg + i * d_per + k, sel, stride=cg), :] = out[:, k * LANES:(k + 1) * LANES]
             return 0
 
-        lax.fori_loop(0, cg * LANES // d_tile, body, 0)
+        lax.fori_loop(0, cg * LANES // d_tile, body, 0, unroll=True)
         half = rg // 2
         snd[g, pl.ds(0, half), :] = acc[span(g * rg + (1 - core) * half, half), :].astype(BF16)
         exchange(rcv_c, c_send, c_recv, g, 0, 1).start()

time: 62.9 us -> 60.6 us (0.963)
  Pallas kernels: 62.1 us -> 59.8 us
    pallas_call x1, Pallas kernels: 60.2 us -> 57.9 us  [shards(): pl.pallas_call(functools.partial(kernel, n_tp, n_lat), out_shape=(jax.Sha...]
where the time goes in v3:
time: 60.6 us; the launch traced here: 60.4 us
  Pallas kernels  59.8 us (99%)
  between operations  0.64 us (1%)
    pallas_call x1, Pallas kernels, shards(): pl.pallas_call(functools.partial(kernel, n_tp, n_lat), out_shape=(jax.Sha...  57.9 us
    pallas_call x1, Pallas kernels, shards(): pl.pallas_call(finish, out_shape=(jax.ShapeDtypeStruct((own_rows, width),...  1.82 us

profile of v3, /device:TPU:0, one launch (start us, length us, event | category | flops | bytes accessed | tf_op | source)
XLA Modules:
  0.0 60.4 jit_solution(15433845175860201048)
XLA Ops:
  0.6 57.9 %shard_map.111 = (bf16[16,8192]{1,0:T(8,128)(2,1)}, bf16[64,1024]{1,0:T(8,128)(2,1)}, f32[128,128]{1,0:T(8,128)}, f32[2,128]{1,0:T(2,128)}) custom-call(s32[1,64]{1,0:T(1,128)} %bitcast.7, bf16[64,512]{1,0:T(8,128)(2,1)} %attn_ref.1, bf16[16,8192]{1,0:T(8,128)(2,1)} %resid_ref.1, f32[1,1024]{1,0:T(1,128)} %bitcast.5, f32[1,1024]{1,0:T(1,128)} %bitcast.6, ...), custom_call_target="tpu_custom_call" | custom-call | flops 3355443200 | bytes 25165824 | tf_op jit(solution)/shard_map/pallas_call | solution.py:363
  58.6 1.8 %shard_map.112 = (bf16[16,8192]{1,0:T(8,128)(2,1)}, bf16[64,1024]{1,0:T(8,128)(2,1)}, bf16[2,8192]{1,0:T(2,128)(2,1)}, f32[2]{0:T(128)}) custom-call(bf16[16,8192]{1,0:T(8,128)(2,1)} %get-tuple-element.8.stream_in, bf16[64,1024]{1,0:T(8,128)(2,1)} %get-tuple-element.9.codes_in, f32[128,128]{1,0:T(8,128)} %get-tuple-element.10.recon_in, ...), custom_call_target="tpu_custom_call" | custom-call | tf_op jit(solution)/shard_map/pallas_call | solution.py:415

commit v4 on v3

--- a/solution.py
+++ b/solution.py
@@ -7,7 +7,7 @@
 from jax.experimental.pallas import tpu as pltpu
 from jax.sharding import PartitionSpec as P
 
-GROUPS = 4
+GROUPS = 2
 LANES = 128
 F32 = jnp.float32
 BF16 = jnp.bfloat16
@@ -394,7 +394,7 @@
             dma((n_tp - 1,)), dma((n_tp - 1,)),
         ],
         compiler_params=pltpu.CompilerParams(
-            collective_id=0, has_side_effects=True, vmem_limit_bytes=60 * 1024 * 1024
+            collective_id=0, has_side_effects=True, vmem_limit_bytes=57 * 1024 * 1024
         ),
         cost_estimate=pl.CostEstimate(
             flops=2 * (2 * sel * width * lats + (rows + sel + own_rows) * depth * width),

time: 60.6 us -> 54.3 us (0.90)
  Pallas kernels: 59.8 us -> 53.5 us
    pallas_call x1, Pallas kernels: 57.9 us -> 51.6 us  [shards(): pl.pallas_call(functools.partial(kernel, n_tp, n_lat), out_shape=(jax.Sha...]
where the time goes in v4:
time: 54.3 us; the launch traced here: 54.1 us
  Pallas kernels  53.5 us (99%)
  between operations  0.64 us (1%)
    pallas_call x1, Pallas kernels, shards(): pl.pallas_call(functools.partial(kernel, n_tp, n_lat), out_shape=(jax.Sha...  51.6 us
    pallas_call x1, Pallas kernels, shards(): pl.pallas_call(finish, out_shape=(jax.ShapeDtypeStruct((own_rows, width),...  1.82 us

profile of v4, /device:TPU:0, one launch (start us, length us, event | category | flops | bytes accessed | tf_op | source)
XLA Modules:
  0.0 54.1 jit_solution(2436084899068711142)
XLA Ops:
  0.6 51.6 %shard_map.111 = (bf16[16,8192]{1,0:T(8,128)(2,1)}, bf16[64,1024]{1,0:T(8,128)(2,1)}, f32[128,128]{1,0:T(8,128)}, f32[2,128]{1,0:T(2,128)}) custom-call(s32[1,64]{1,0:T(1,128)} %bitcast.7, bf16[64,512]{1,0:T(8,128)(2,1)} %attn_ref.1, bf16[16,8192]{1,0:T(8,128)(2,1)} %resid_ref.1, f32[1,1024]{1,0:T(1,128)} %bitcast.5, f32[1,1024]{1,0:T(1,128)} %bitcast.6, ...), custom_call_target="tpu_custom_call" | custom-call | flops 3355443200 | bytes 25165824 | tf_op jit(solution)/shard_map/pallas_call | solution.py:363
  52.3 1.8 %shard_map.112 = (bf16[16,8192]{1,0:T(8,128)(2,1)}, bf16[64,1024]{1,0:T(8,128)(2,1)}, bf16[2,8192]{1,0:T(2,128)(2,1)}, f32[2]{0:T(128)}) custom-call(bf16[16,8192]{1,0:T(8,128)(2,1)} %get-tuple-element.8.stream_in, bf16[64,1024]{1,0:T(8,128)(2,1)} %get-tuple-element.9.codes_in, f32[128,128]{1,0:T(8,128)} %get-tuple-element.10.recon_in, ...), custom_call_target="tpu_custom_call" | custom-call | tf_op jit(solution)/shard_map/pallas_call | solution.py:415

commit v5 on v4

--- a/solution.py
+++ b/solution.py
@@ -216,16 +216,27 @@
 
         lax.fori_loop(0, pre.shape[1] // n_tile, body, 0, unroll=True)
 
-    def mix(d):
+    mix_parts = (pl.ds(0, width // 4), pl.ds(width // 4, width - width // 4))
+
+    def mix(part, d):
         to = mix_peer(d)
+        sem = part * (n_tp - 1) + d - 1
         return pltpu.make_async_remote_copy(
-            src_ref=mix_snd.at[pl.ds(pl.multiple_of(to * own_rows, own_rows), own_rows), :],
-            dst_ref=mix_rcv.at[d - 1],
-            send_sem=m_send.at[d - 1],
-            recv_sem=m_recv.at[d - 1],
+            src_ref=mix_snd.at[pl.ds(pl.multiple_of(to * own_rows, own_rows), own_rows), mix_parts[part]],
+            dst_ref=mix_rcv.at[d - 1, :, mix_parts[part]],
+            send_sem=m_send.at[sem],
+            recv_sem=m_recv.at[sem],
             device_id={"tp": to},
             device_id_type=MESH,
         )
+
+    def mix_start(part):
+        for d in range(1, n_tp):
+            mix(part, d).start()
+
+    def mix_early(t):
+        if t == GROUPS + 2:
+            mix_start(0)
 
     def wave(ops, after=None):
         for t in range(len(ops) + GROUPS - 1):
@@ -239,8 +250,7 @@
         share_take(g, 1)
         share_start(g, 0)
         if g == GROUPS - 1:
-            for d in range(1, n_tp):
-                mix(d).start()
+            mix_start(1)
         if g == 0:
             for one in enc_loads:
                 one.wait()
@@ -251,6 +261,8 @@
         encode(g, (1 - core) * (rg // 2), rg // 2)
 
     def pass_on(g, s):
+        if g == GROUPS - 1 and s == n_steps - 1:
+            sent(rcv_a, a_send, a_recv)
         share_take(g, s)
         share_start(g, s - 1)
 
@@ -259,12 +271,7 @@
     ops += [functools.partial(take, rcv_a, a_send, a_recv, own_rows_done, s=s) for s in range(n_steps)]
     ops += [functools.partial(pass_on, s=s) for s in reversed(range(2, n_steps))]
     ops += [encode_near, encode_far]
-    wave(ops)
-    sent(rcv_a, a_send, a_recv)
-    for g in range(GROUPS):
-        for s in range(n_steps):
-            for d in range(1, steps[s][2]):
-                share(g, s, d).wait_send()
+    wave(ops, mix_early)
 
     codes = (jnp.maximum(pre[...] + b_enc_ref[...], 0.0) * norm_ref[...]).astype(BF16)
     codes_ref[...] = codes
@@ -284,7 +291,9 @@
     d_tile = min(256, cg * LANES)
     d_per = d_tile // LANES
 
-    def decode(g):
+    d_count = cg * LANES // d_tile
+
+    def decode(g, low, high):
         left = cperm[...]
 
         def body(i, _):
@@ -294,7 +303,9 @@
                 acc[pl.ds(g * rg + i * d_per + k, sel, stride=cg), :] = out[:, k * LANES:(k + 1) * LANES]
             return 0
 
-        lax.fori_loop(0, cg * LANES // d_tile, body, 0, unroll=True)
+        lax.fori_loop(low, high, body, 0, unroll=True)
+        if high < d_count:
+            return
         half = rg // 2
         snd[g, pl.ds(0, half), :] = acc[span(g * rg + (1 - core) * half, half), :].astype(BF16)
         exchange(rcv_c, c_send, c_recv, g, 0, 1).start()
@@ -308,11 +319,10 @@
             off = full - mine[r, g * cg:(g + 1) * cg, :]
             sums[r] = off * off if sums[r] is None else sums[r] + off * off
 
-    def keep_stream(t):
-        if t != GROUPS:
-            return
-        for d in range(1, n_tp):
-            mix(d).wait_recv()
+    def keep_stream():
+        for part in range(len(mix_parts)):
+            for d in range(1, n_tp):
+                mix(part, d).wait_recv()
 
         def body(i, _):
             cols = pl.ds(pl.multiple_of(i * 1024, 1024), 1024)
@@ -324,14 +334,29 @@
 
         lax.fori_loop(0, width // 1024, body, 0)
 
-    ops = [decode] + [functools.partial(take, rcv_c, c_send, c_recv, score, s=s) for s in range(n_steps)]
-    wave(ops, keep_stream)
+    take_c = functools.partial(take, rcv_c, c_send, c_recv, score)
+    decode(0, 0, d_count)
+    for g in range(1, GROUPS):
+        decode(g, 0, d_count // 2)
+        take_c(g - 1, 0)
+        decode(g, d_count // 2, d_count)
+    take_c(GROUPS - 1, 0)
+    for s in range(1, n_steps):
+        if s == n_steps - 1:
+            keep_stream()
+        for g in range(GROUPS):
+            take_c(g, s)
     for r in range(keep):
         total = jnp.sum(jnp.sum(sums[r], axis=0, keepdims=True), axis=1, keepdims=True) / width
         err_ref[r:r + 1, :] = jnp.broadcast_to(total, (1, LANES))
     sent(rcv_c, c_send, c_recv)
-    for d in range(1, n_tp):
-        mix(d).wait_send()
+    for g in range(GROUPS):
+        for s in range(n_steps):
+            for d in range(1, steps[s][2]):
+                share(g, s, d).wait_send()
+    for part in range(len(mix_parts)):
+        for d in range(1, n_tp):
+            mix(part, d).wait_send()
 
 
 def finish(stream_in, codes_in, recon_in, err_in, stream_ref, codes_ref, recon_ref, err_ref):
@@ -391,7 +416,7 @@
             dma((n_sem,)), dma((n_sem,)),
             dma((n_sem,)), dma((n_sem,)),
             dma((n_sem,)), dma((n_sem,)),
-            dma((n_tp - 1,)), dma((n_tp - 1,)),
+            dma((2 * (n_tp - 1),)), dma((2 * (n_tp - 1),)),
         ],
         compiler_params=pltpu.CompilerParams(
             collective_id=0, has_side_effects=True, vmem_limit_bytes=57 * 1024 * 1024

time: 54.3 us -> 53.2 us (0.980)
  Pallas kernels: 53.5 us -> 52.4 us
    pallas_call x1, Pallas kernels: 51.6 us -> 50.5 us  [shards(): pl.pallas_call(functools.partial(kernel, n_tp, n_lat), out_shape=(jax.Sha...]
where the time goes in v5:
time: 53.2 us; the launch traced here: 53 us
  Pallas kernels  52.4 us (98%)
  between operations  0.64 us (1%)
    pallas_call x1, Pallas kernels, shards(): pl.pallas_call(functools.partial(kernel, n_tp, n_lat), out_shape=(jax.Sha...  50.5 us
    pallas_call x1, Pallas kernels, shards(): pl.pallas_call(finish, out_shape=(jax.ShapeDtypeStruct((own_rows, width),...  1.82 us

profile of v5, /device:TPU:0, one launch (start us, length us, event | category | flops | bytes accessed | tf_op | source)
XLA Modules:
  0.0 53.0 jit_solution(16040263315208789522)
XLA Ops:
  0.6 50.5 %shard_map.111 = (bf16[16,8192]{1,0:T(8,128)(2,1)}, bf16[64,1024]{1,0:T(8,128)(2,1)}, f32[128,128]{1,0:T(8,128)}, f32[2,128]{1,0:T(2,128)}) custom-call(s32[1,64]{1,0:T(1,128)} %bitcast.7, bf16[64,512]{1,0:T(8,128)(2,1)} %attn_ref.1, bf16[16,8192]{1,0:T(8,128)(2,1)} %resid_ref.1, f32[1,1024]{1,0:T(1,128)} %bitcast.5, f32[1,1024]{1,0:T(1,128)} %bitcast.6, ...), custom_call_target="tpu_custom_call" | custom-call | flops 3355443200 | bytes 25165824 | tf_op jit(solution)/shard_map/pallas_call | solution.py:388
  51.2 1.8 %shard_map.112 = (bf16[16,8192]{1,0:T(8,128)(2,1)}, bf16[64,1024]{1,0:T(8,128)(2,1)}, bf16[2,8192]{1,0:T(2,128)(2,1)}, f32[2]{0:T(128)}) custom-call(bf16[16,8192]{1,0:T(8,128)(2,1)} %get-tuple-element.8.stream_in, bf16[64,1024]{1,0:T(8,128)(2,1)} %get-tuple-element.9.codes_in, f32[128,128]{1,0:T(8,128)} %get-tuple-element.10.recon_in, ...), custom_call_target="tpu_custom_call" | custom-call | tf_op jit(solution)/shard_map/pallas_call | solution.py:440

commit v6 on v5

--- a/solution.py
+++ b/solution.py
@@ -70,10 +70,8 @@
         cols = pl.ds(piece(g, which), half_cols)
         return pltpu.make_async_copy(w_out_hbm.at[:, cols], w_out.at[:, cols], in_sem.at[which * GROUPS + g])
 
-    load(0, 0).start()
     for g in range(GROUPS):
-        if g + 1 < GROUPS:
-            load(g + 1, 0).start()
+        load(g, 0).start()
         load(g, 1).start()
     n_enc = enc_sem.shape[0]
     enc_rows = width // n_enc
@@ -235,7 +233,7 @@
             mix(part, d).start()
 
     def mix_early(t):
-        if t == GROUPS + 2:
+        if t == GROUPS:
             mix_start(0)
 
     def wave(ops, after=None):
@@ -267,8 +265,18 @@
         share_start(g, s - 1)
 
     pre[...] = jnp.zeros_like(pre)
-    ops = [functools.partial(project, which=0), functools.partial(project, which=1)]
-    ops += [functools.partial(take, rcv_a, a_send, a_recv, own_rows_done, s=s) for s in range(n_steps)]
+    take_a = functools.partial(take, rcv_a, a_send, a_recv, own_rows_done)
+    for g in range(GROUPS):
+        project(g, 0)
+        if g > 0:
+            take_a(g - 1, 0)
+        project(g, 1)
+
+    def take_last(g):
+        if g == GROUPS - 1:
+            take_a(g, 0)
+
+    ops = [take_last] + [functools.partial(take_a, s=s) for s in range(1, n_steps)]
     ops += [functools.partial(pass_on, s=s) for s in reversed(range(2, n_steps))]
     ops += [encode_near, encode_far]
     wave(ops, mix_early)

time: 53.2 us -> 51.8 us (0.974)
  Pallas kernels: 52.4 us -> 51 us
    pallas_call x1, Pallas kernels: 50.5 us -> 49.2 us  [shards(): pl.pallas_call(functools.partial(kernel, n_tp, n_lat), out_shape=(jax.Sha...]
where the time goes in v6:
time: 51.8 us; the launch traced here: 51.7 us
  Pallas kernels  51 us (98%)
  between operations  0.64 us (1%)
    pallas_call x1, Pallas kernels, shards(): pl.pallas_call(functools.partial(kernel, n_tp, n_lat), out_shape=(jax.Sha...  49.2 us
    pallas_call x1, Pallas kernels, shards(): pl.pallas_call(finish, out_shape=(jax.ShapeDtypeStruct((own_rows, width),...  1.82 us

profile of v6, /device:TPU:0, one launch (start us, length us, event | category | flops | bytes accessed | tf_op | source)
XLA Modules:
  0.0 51.7 jit_solution(16739338827578431674)
XLA Ops:
  0.6 49.2 %shard_map.111 = (bf16[16,8192]{1,0:T(8,128)(2,1)}, bf16[64,1024]{1,0:T(8,128)(2,1)}, f32[128,128]{1,0:T(8,128)}, f32[2,128]{1,0:T(2,128)}) custom-call(s32[1,64]{1,0:T(1,128)} %bitcast.7, bf16[64,512]{1,0:T(8,128)(2,1)} %attn_ref.1, bf16[16,8192]{1,0:T(8,128)(2,1)} %resid_ref.1, f32[1,1024]{1,0:T(1,128)} %bitcast.5, f32[1,1024]{1,0:T(1,128)} %bitcast.6, ...), custom_call_target="tpu_custom_call" | custom-call | flops 3355443200 | bytes 25165824 | tf_op jit(solution)/shard_map/pallas_call | solution.py:396
  49.9 1.8 %shard_map.112 = (bf16[16,8192]{1,0:T(8,128)(2,1)}, bf16[64,1024]{1,0:T(8,128)(2,1)}, bf16[2,8192]{1,0:T(2,128)(2,1)}, f32[2]{0:T(128)}) custom-call(bf16[16,8192]{1,0:T(8,128)(2,1)} %get-tuple-element.8.stream_in, bf16[64,1024]{1,0:T(8,128)(2,1)} %get-tuple-element.9.codes_in, f32[128,128]{1,0:T(8,128)} %get-tuple-element.10.recon_in, ...), custom_call_target="tpu_custom_call" | custom-call | tf_op jit(solution)/shard_map/pallas_call | solution.py:448
